TPU v7x, 32 devices: a whole 2x2x4 slice. The times are simulated.
32 devices in a mesh: seq: 16 (over z, y, x), tp: 2 (over core).
Axes of the slice: x: 2, y: 2, z: 4, core: 2. Of those that a mesh axis runs over, the one named last changes fastest.
Arguments:
- queries: bfloat16 [4096, 4096], P('seq', 'tp'), may hold values from -50 to 50
- keys: bfloat16 [4096, 4096], P('seq', 'tp'), may hold values from -4 to 4
- values: bfloat16 [4096, 4096], P('seq', 'tp'), may hold values from -18 to 18
- doc_lengths: int32 [32], replicated, may hold values from 1 to 2048, 4096 in all
- out_weight: bfloat16 [4096, 4096], P('tp', 'seq'), may hold values from -0.125 to 0.125
Outputs:
- projected: bfloat16 [4096, 4096], P('seq', 'tp')
Inputs may be any that keep to these rules, and one draw needn't show every extreme that they name: `doc_lengths`: document lengths in order, summing to 4096; the longest is exactly 2048.
All inputs are finite; a program needn't handle non-finite values.
Results may differ from a plain program's by a relative error of at most 0.015.
Values may be sent and summed in bfloat16 or wider, within the bound.
A program may use at most 128 MiB of HBM per device.

v0:
```python
import math

import jax
import jax.numpy as jnp
from jax import lax
from jax.sharding import PartitionSpec as P

HD = 128


def doc_of(positions, doc_lengths):
    ends = jnp.cumsum(doc_lengths)
    return jnp.sum((ends[None, :] <= positions[:, None]).astype(jnp.int32), axis=1)


def absorb(carry, query_heads, query_ids, key_heads, value_heads, key_ids):
    run_max, run_sum, accum = carry
    scale = 1.0 / math.sqrt(HD)
    scores = (
        jnp.einsum("qhd,khd->hqk", query_heads, key_heads, preferred_element_type=jnp.float32)
        * scale
    )
    same = (query_ids[:, None] == key_ids[None, :])[None]
    scores = jnp.where(same, scores, -1e30)
    new_max = jnp.maximum(run_max, jnp.max(scores, axis=2))
    weights = jnp.where(same, jnp.exp(scores - new_max[:, :, None]), 0.0)
    factor = jnp.exp(run_max - new_max)
    run_sum = run_sum * factor + jnp.sum(weights, axis=2)
    accum = accum * factor[:, :, None] + jnp.einsum(
        "hqk,khd->hqd",
        weights.astype(jnp.bfloat16),
        value_heads,
        preferred_element_type=jnp.float32,
    )
    return (new_max, run_sum, accum)


def local(queries, keys, values, doc_lengths, out_weight):
    rows = queries.shape[0]
    heads_here = queries.shape[1] // HD
    index = lax.axis_index("seq")
    query_heads = queries.reshape(rows, heads_here, HD)
    query_ids = doc_of(index * rows + jnp.arange(rows, dtype=jnp.int32), doc_lengths)

    def absorb_block(carry, key_rows, value_rows, key_ids):
        key_heads = key_rows.reshape(key_rows.shape[0], heads_here, HD)
        value_heads = value_rows.reshape(value_rows.shape[0], heads_here, HD)
        return absorb(carry, query_heads, query_ids, key_heads, value_heads, key_ids)

    start_state = (
        jnp.full((heads_here, rows), -1e30, jnp.float32),
        jnp.zeros((heads_here, rows), jnp.float32),
        jnp.zeros((heads_here, rows, HD), jnp.float32),
    )
    piece_keys = lax.all_gather(keys, "seq", axis=0, tiled=True)
    piece_values = lax.all_gather(values, "seq", axis=0, tiled=True)
    piece_rows = piece_keys.shape[0]
    span = 2 * rows

    def step_block(number, state):
        offset = number * span
        block_keys = lax.dynamic_slice_in_dim(piece_keys, offset, span, 0)
        block_values = lax.dynamic_slice_in_dim(piece_values, offset, span, 0)
        block_ids = doc_of(offset + jnp.arange(span, dtype=jnp.int32), doc_lengths)
        return absorb_block(state, block_keys, block_values, block_ids)

    final_state = lax.fori_loop(0, piece_rows // span, step_block, start_state)
    run_max, run_sum, accum = final_state
    mixed = accum / run_sum[:, :, None]
    attended = jnp.transpose(mixed, (1, 0, 2)).reshape(rows, heads_here * HD).astype(jnp.bfloat16)
    partial_value = jnp.dot(
        attended,
        lax.all_gather(out_weight, "seq", axis=1, tiled=True),
        preferred_element_type=jnp.float32,
    )
    return lax.psum_scatter(
        partial_value.astype(jnp.bfloat16), "tp", scatter_dimension=1, tiled=True
    )


def solution(mesh):
    in_specs = (P("seq", "tp"), P("seq", "tp"), P("seq", "tp"), P(), P("tp", "seq"))
    out_specs = P("seq", "tp")
    return jax.shard_map(local, mesh=mesh, in_specs=in_specs, out_specs=out_specs, check_vma=False)
```

profile of v0, /device:TPU:25, one launch (start us, length us, event | category | flops | bytes accessed | tf_op | source)
XLA Modules:
  0.0 745.5 jit_solution(15662900539599789899)
XLA Ops:
  15.1 228.4 %all-gather.4.cloned.1.call-done = bf16[4096,2048]{0,1:T(8,128)(2,1)} async-done(((bf16[256,2048]{0,1:T(8,128)(2,1)}), bf16[4096,2048]{0,1:T(8,128)(2,1)}) %all-gather.4.cloned.1.call-update) | async-done | bytes 16777232 | tf_op jit(solution)/shard_map/all_gather | solution.py:55
  243.5 236.2 %all-gather.6.cloned.1.call-done = bf16[4096,2048]{0,1:T(8,128)(2,1)} async-done(((bf16[256,2048]{0,1:T(8,128)(2,1)}), bf16[4096,2048]{0,1:T(8,128)(2,1)}) %all-gather.6.cloned.1.call-update) | async-done | bytes 16777232 | tf_op jit(solution)/shard_map/all_gather | solution.py:56
  479.7 154.2 %while.20 = (s32[]{:T(128)}, f32[16,256]{1,0:T(8,128)S(1)}, f32[16,256]{1,0:T(8,128)S(1)}, f32[16,256,128]{2,1,0:T(8,128)}, s32[256]{0:T(256)S(1)}, /*index=5*/s...) while((s32[]{:T(128)}, f32[16,256]{1,0:T(8,128)S(1)}, ...), condition=%wide.region_6.7_spmd.clone, body=%wide.region_2.6_spmd.clone.sunk | while | flops 1102778368 | bytes 77342040 | solution.py:67
  482.5 4.8 fusion.30
  487.3 4.6 fusion.31
  493.7 4.4 fusion.33
  500.8 4.8 fusion.30
  505.7 4.7 fusion.31
  511.6 5.6 fusion.33
  520.0 4.8 fusion.30
  524.8 5.1 fusion.31
  531.5 5.6 fusion.33
  539.8 4.8 fusion.30
  544.7 4.6 fusion.31
  550.5 5.6 fusion.33
  556.1 2.5 constant_dynamic-slice_fusion.3
  558.9 4.8 fusion.30
  563.7 4.7 fusion.31
  569.6 5.6 fusion.33
  578.0 5.0 fusion.30
  583.0 5.2 fusion.31
  590.0 5.6 fusion.33
  598.4 4.8 fusion.30
  603.2 4.7 fusion.31
  609.2 5.6 fusion.33
  614.8 2.5 constant_dynamic-slice_fusion.3
  617.6 4.8 fusion.30
  622.4 4.6 fusion.31
  628.3 5.6 fusion.33
  636.0 79.8 %all-gather.8.cloned.1.call-done = bf16[2048,4096]{1,0:T(8,128)(2,1)} async-done(((bf16[2048,256]{1,0:T(8,128)(2,1)}), bf16[2048,4096]{1,0:T(8,128)(2,1)}) %all-gather.8.cloned.1.call-update) | async-done | bytes 16777232 | tf_op jit(solution)/shard_map/all_gather | solution.py:73
  715.9 11.6 %convolution_convert_fusion = bf16[256,4096]{1,0:T(8,128)(2,1)} fusion(bf16[256,2048]{0,1:T(8,128)(2,1)S(1)} %bitcast.47, bf16[2048,4096]{1,0:T(8,128)(2,1)} %all-gather.8.cloned.1.call-done), kind=kOutput, calls=%fused_computation.21 | convolution fusion | flops 4296015872 | bytes 19922944 | tf_op jit(solution)/shard_map/dot_general | solution.py:71
  727.5 11.5 %reduce-scatter.2.cloned.1.call-done = bf16[256,2048]{1,0:T(8,128)(2,1)} async-done(((bf16[256,4096]{1,0:T(8,128)(2,1)}), bf16[256,2048]{1,0:T(8,128)(2,1)}) %reduce-scatter.2.cloned.1.call-update) | async-done | bytes 1048592 | tf_op jit(solution)/shard_map/reduce_scatter | solution.py:76
  (90 shorter events, 38.9 us)
Async XLA Ops:
  6.5 237.0 %all-gather.4.cloned.1.call-start = ((), (), s32[]{:S(2)}) async-start(), calls=%async_computation.1 | async-start | bytes 17825792 | tf_op jit(solution)/shard_map/all_gather | solution.py:55
  8.8 470.9 %all-gather.6.cloned.1.call-start = ((), (), s32[]{:S(2)}) async-start(), calls=%async_computation.2 | async-start | bytes 17825792 | tf_op jit(solution)/shard_map/all_gather | solution.py:56
  11.2 704.7 %all-gather.8.cloned.1.call-start = ((), (), s32[]{:S(2)}) async-start(), calls=%async_computation.3 | async-start | bytes 17825792 | tf_op jit(solution)/shard_map/all_gather | solution.py:73
  11.9 727.0 %reduce-scatter.2.cloned.1.call-start = ((), (), s32[]{:S(2)}) async-start(), calls=%async_computation.4 | async-start | bytes 3145728 | tf_op jit(solution)/shard_map/reduce_scatter | solution.py:76
  487.3 6.4 copy-start
  505.7 5.9 copy-start
  524.8 6.7 copy-start
  544.7 5.8 copy-start
  563.7 5.9 copy-start
  583.0 7.0 copy-start
  603.2 6.0 copy-start
  622.4 5.9 copy-start
Sparse Core Ops, SparseCore 0:
  10.1 233.3 all-gather.3
  246.2 233.4 all-gather.5
  482.4 233.4 all-gather.7
  727.6 11.3 reduce-scatter.1
where the time goes:
time: 747 us; the launch traced here: 745 us
  waiting for transfers between devices  557 us (75%)
  matrix products  94 us (13%)
  other arithmetic  41.4 us (6%)
  local copies, waits for them, and re-layouts  39.9 us (5%)
  between operations  13.2 us (2%)
    all_gather x1, waiting for transfers between devices, local(): piece_values = lax.all_gather(values, 'seq', axis=0, tiled=True)  236 us
    all_gather x1, waiting for transfers between devices, local(): piece_keys = lax.all_gather(keys, 'seq', axis=0, tiled=True)  228 us
    all_gather x1, waiting for transfers between devices, local(): lax.all_gather(out_weight, 'seq', axis=1, tiled=True)  79.8 us
    dot_general x8, matrix products, absorb(): jnp.einsum('hqk,khd->hqd', weights.astype(jnp.bfloat16), value_heads, pre...  43.5 us
    dot_general x8, matrix products, absorb(): jnp.einsum('qhd,khd->hqk', query_heads, key_heads, preferred_element_type...  38.9 us
    reduce_sum x8, other arithmetic, absorb(): run_sum = run_sum * factor + jnp.sum(weights, axis=2)  38.2 us
    dynamic_slice x8, local copies, waits for them, and re-layouts, step_block(): block_values = lax.dynamic_slice_in_dim(piece_values, offset, span, 0)  20.1 us
  transfers between devices with their start and end apart: 4, of which 4 were waited for; matrix products, arithmetic and copies ran while one was open for 20% of the time, Pallas kernels for 0%

commit v1 on v0

--- a/solution.py
+++ b/solution.py
@@ -1,15 +1,25 @@
+import functools
 import math
 
 import jax
 import jax.numpy as jnp
 from jax import lax
+from jax.experimental import pallas as pl
+from jax.experimental.pallas import tpu as pltpu
 from jax.sharding import PartitionSpec as P
 
 HD = 128
+SCALE2 = math.log2(math.e) / math.sqrt(HD)
+
+
+def ends_of(doc_lengths):
+    count = doc_lengths.shape[0]
+    before = jnp.arange(count)[None, :] <= jnp.arange(count)[:, None]
+    return jnp.sum(jnp.where(before, doc_lengths[None, :], 0), axis=1)
 
 
 def doc_of(positions, doc_lengths):
-    ends = jnp.cumsum(doc_lengths)
+    ends = ends_of(doc_lengths)
     return jnp.sum((ends[None, :] <= positions[:, None]).astype(jnp.int32), axis=1)
 
 
@@ -35,7 +45,7 @@
     return (new_max, run_sum, accum)
 
 
-def local(queries, keys, values, doc_lengths, out_weight):
+def attend_gathered(queries, keys, values, doc_lengths):
     rows = queries.shape[0]
     heads_here = queries.shape[1] // HD
     index = lax.axis_index("seq")
@@ -64,15 +74,99 @@
         block_ids = doc_of(offset + jnp.arange(span, dtype=jnp.int32), doc_lengths)
         return absorb_block(state, block_keys, block_values, block_ids)
 
-    final_state = lax.fori_loop(0, piece_rows // span, step_block, start_state)
-    run_max, run_sum, accum = final_state
+    run_max, run_sum, accum = lax.fori_loop(0, piece_rows // span, step_block, start_state)
     mixed = accum / run_sum[:, :, None]
-    attended = jnp.transpose(mixed, (1, 0, 2)).reshape(rows, heads_here * HD).astype(jnp.bfloat16)
-    partial_value = jnp.dot(
-        attended,
-        lax.all_gather(out_weight, "seq", axis=1, tiled=True),
-        preferred_element_type=jnp.float32,
+    return jnp.transpose(mixed, (1, 0, 2)).reshape(rows, heads_here * HD).astype(jnp.bfloat16)
+
+
+def attend_kernel(bk, low_ref, high_ref, q_ref, k_ref, v_ref, qid_ref, kid_ref, o_ref):
+    bq = q_ref.shape[0]
+    i = pl.program_id(1)
+    own = (i * bq) // bk
+    q = q_ref[...]
+    qid = qid_ref[...]
+
+    def part(j):
+        start = pl.multiple_of(j * bk, bk)
+        s = lax.dot_general(
+            q, k_ref[pl.ds(start, bk), :], (((1,), (1,)), ((), ())),
+            preferred_element_type=jnp.float32,
+        )
+        kid = kid_ref[j]
+        s = jnp.where(qid == kid, s, -1e30)
+        return s, v_ref[pl.ds(start, bk), :]
+
+    s, v = part(own)
+    m = jnp.max(s, axis=1, keepdims=True)
+    p = jnp.exp2((s - m) * SCALE2)
+    total = jnp.sum(p, axis=1, keepdims=True)
+    acc = jnp.dot(p.astype(jnp.bfloat16), v, preferred_element_type=jnp.float32)
+
+    def step(n, state):
+        m, total, acc = state
+        j = jnp.where(n >= own, n + 1, n)
+        s, v = part(j)
+        new = jnp.maximum(m, jnp.max(s, axis=1, keepdims=True))
+        p = jnp.exp2((s - new) * SCALE2)
+        factor = jnp.exp2((m - new) * SCALE2)
+        total = total * factor + jnp.sum(p, axis=1, keepdims=True)
+        acc = acc * factor + jnp.dot(
+            p.astype(jnp.bfloat16), v, preferred_element_type=jnp.float32
+        )
+        return new, total, acc
+
+    m, total, acc = lax.fori_loop(low_ref[i], high_ref[i], step, (m, total, acc))
+    o_ref[...] = (acc / total).astype(o_ref.dtype)
+
+
+def attend_heads(q, k, v, doc_lengths):
+    tokens, width = q.shape
+    bq = math.gcd(tokens, 256)
+    bk = math.gcd(tokens, 512)
+    ids = doc_of(jnp.arange(tokens, dtype=jnp.int32), doc_lengths)
+    ends = ends_of(doc_lengths)
+    starts = ends - doc_lengths
+    firsts = jnp.arange(tokens // bq, dtype=jnp.int32) * bq
+    lasts = firsts + bq - 1
+    low = jnp.max(jnp.where(starts[None, :] <= firsts[:, None], starts[None, :], 0), axis=1) // bk
+    high = (jnp.min(jnp.where(ends[None, :] > lasts[:, None], ends[None, :], tokens), axis=1) - 1) // bk
+    grid_spec = pltpu.PrefetchScalarGridSpec(
+        num_scalar_prefetch=2,
+        grid=(width // HD, tokens // bq),
+        in_specs=[
+            pl.BlockSpec((bq, HD), lambda h, i, *_: (i, h)),
+            pl.BlockSpec((tokens, HD), lambda h, i, *_: (0, h)),
+            pl.BlockSpec((tokens, HD), lambda h, i, *_: (0, h)),
+            pl.BlockSpec((bq, 1), lambda h, i, *_: (i, 0)),
+            pl.BlockSpec((tokens // bk, 1, bk), lambda h, i, *_: (0, 0, 0)),
+        ],
+        out_specs=pl.BlockSpec((bq, HD), lambda h, i, *_: (i, h)),
     )
+    return pl.pallas_call(
+        functools.partial(attend_kernel, bk),
+        out_shape=jax.ShapeDtypeStruct((tokens, width), jnp.bfloat16),
+        grid_spec=grid_spec,
+        compiler_params=pltpu.CompilerParams(vmem_limit_bytes=32 << 20),
+        cost_estimate=pl.CostEstimate(
+            flops=tokens * tokens * width * 2, bytes_accessed=tokens * width * 8,
+            transcendentals=tokens * tokens * width // HD // 2,
+        ),
+    )(low, high, q, k, v, ids[:, None], ids.reshape(tokens // bk, 1, bk))
+
+
+def local(parts, queries, keys, values, doc_lengths, out_weight):
+    heads_here = queries.shape[1] // HD
+    weight = lax.all_gather(out_weight, "seq", axis=1, tiled=True)
+    if heads_here % parts == 0:
+        q, k, v = [
+            lax.all_to_all(a, "seq", split_axis=1, concat_axis=0, tiled=True)
+            for a in (queries, keys, values)
+        ]
+        mixed = attend_heads(q, k, v, doc_lengths)
+        attended = lax.all_to_all(mixed, "seq", split_axis=0, concat_axis=1, tiled=True)
+    else:
+        attended = attend_gathered(queries, keys, values, doc_lengths)
+    partial_value = jnp.dot(attended, weight, preferred_element_type=jnp.float32)
     return lax.psum_scatter(
         partial_value.astype(jnp.bfloat16), "tp", scatter_dimension=1, tiled=True
     )
@@ -81,4 +175,7 @@
 def solution(mesh):
     in_specs = (P("seq", "tp"), P("seq", "tp"), P("seq", "tp"), P(), P("tp", "seq"))
     out_specs = P("seq", "tp")
-    return jax.shard_map(local, mesh=mesh, in_specs=in_specs, out_specs=out_specs, check_vma=False)
+    return jax.shard_map(
+        functools.partial(local, mesh.shape["seq"]),
+        mesh=mesh, in_specs=in_specs, out_specs=out_specs, check_vma=False,
+    )

time: 747 us -> 341 us (0.46)
  waiting for transfers between devices: 557 us -> 188 us
  matrix products: 94 us -> 11.5 us
  blocking collectives: 0 us -> 64.3 us
  other arithmetic: 41.4 us -> 1.97 us
  local copies, waits for them, and re-layouts: 39.9 us -> 12.3 us
  Pallas kernels: 0 us -> 25.8 us
  starting transfers between devices: 0.12 us -> 22.7 us
    all_gather x3 -> x1, waiting for transfers between devices: 544 us -> 73.9 us  [local(): weight = lax.all_gather(out_weight, 'seq', axis=1, tiled=True)]
    all_to_all x0 -> x3, waiting for transfers between devices: none -> 102 us  [local(): lax.all_to_all(a, 'seq', split_axis=1, concat_axis=0, tiled=True)]
    dot_general x17 -> x1, matrix products: 94 us -> 11.5 us  [local(): jnp.dot(attended, weight, preferred_element_type=jnp.float32)]
    all_to_all x0 -> x1, blocking collectives: none -> 64.3 us  [local(): lax.all_to_all(mixed, 'seq', split_axis=0, concat_axis=1, tiled=True)]
    reduce_sum x8 -> x1, other arithmetic: 38.2 us -> 0.77 us  [ends_of(): return jnp.sum(jnp.where(before, doc_lengths[None, :], 0), axis=1)]
    pallas_call x0 -> x1, Pallas kernels: none -> 25.8 us  [attend_heads(): pl.pallas_call(functools.partial(attend_kernel, bk), out_shape=jax.ShapeD...]
    all_to_all x0 -> x3, starting transfers between devices: none -> 22.6 us  [local(): lax.all_to_all(a, 'seq', split_axis=1, concat_axis=0, tiled=True)]
    dynamic_slice x8 -> x0, local copies, waits for them, and re-layouts: 20.1 us -> none  [step_block(): block_values = lax.dynamic_slice_in_dim(piece_values, offset, span, 0)]
  transfers between devices with their start and end apart: 4 -> 5, of which waited for: 4 -> 5; matrix products, arithmetic and copies ran while one was open for 20% -> 3% of each run, Pallas kernels for 0% -> 8%
where the time goes in v1:
time: 341 us; the launch traced here: 340 us
  waiting for transfers between devices  188 us (55%)
  blocking collectives  64.3 us (19%)
  Pallas kernels  25.8 us (8%)
  starting transfers between devices  22.7 us (7%)
  between operations  13.5 us (4%)
  local copies, waits for them, and re-layouts  12.3 us (4%)
  matrix products  11.5 us (3%)
    all_to_all x3, waiting for transfers between devices, local(): lax.all_to_all(a, 'seq', split_axis=1, concat_axis=0, tiled=True)  102 us
    all_gather x1, waiting for transfers between devices, local(): weight = lax.all_gather(out_weight, 'seq', axis=1, tiled=True)  73.9 us
    all_to_all x1, blocking collectives, local(): lax.all_to_all(mixed, 'seq', split_axis=0, concat_axis=1, tiled=True)  64.3 us
    pallas_call x1, Pallas kernels, attend_heads(): pl.pallas_call(functools.partial(attend_kernel, bk), out_shape=jax.ShapeD...  25.8 us
    all_to_all x3, starting transfers between devices, local(): lax.all_to_all(a, 'seq', split_axis=1, concat_axis=0, tiled=True)  22.6 us
    dot_general x1, matrix products, local(): jnp.dot(attended, weight, preferred_element_type=jnp.float32)  11.5 us
    reduce_scatter x1, waiting for transfers between devices, local(): lax.psum_scatter(partial_value.astype(jnp.bfloat16), 'tp', scatter_dimens...  11.3 us
  transfers between devices with their start and end apart: 5, of which 5 were waited for; matrix products, arithmetic and copies ran while one was open for 3% of the time, Pallas kernels for 8%

profile of v1, /device:TPU:25, one launch (start us, length us, event | category | flops | bytes accessed | tf_op | source)
XLA Modules:
  0.0 340.3 jit_solution(13390094957122193842)
XLA Ops:
  6.5 0.0 copy-start
  6.5 0.0 all-gather.2.cloned.1.call-start
  6.5 0.7 all-gather.2.cloned.1.call-update
  7.3 0.5 copy-done
  7.8 1.2 copy_bitcast_fusion.2
  9.0 6.4 %all-to-all-start = ((bf16[256,16,128]{2,0,1:T(8,128)(2,1)}), bf16[256,16,128]{2,0,1:T(8,128)(2,1)S(1)}, u32[]{:S(2)}, u32[]{:S(2)}) async-start(bf16[256,16,128]{2,0,1:T(8,128)(2,1)} %copy_bitcast_fusion.2), calls=%async_computation | async-start | bytes 2097152 | tf_op jit(solution)/shard_map/all_to_all | solution.py:162
  15.4 2.5 copy_bitcast_fusion.1
  18.0 33.5 %all-to-all-done = bf16[256,16,128]{2,0,1:T(8,128)(2,1)S(1)} async-done(((bf16[256,16,128]{2,0,1:T(8,128)(2,1)}), bf16[256,16,128]{2,0,1:T(8,128)(2,1)S(1)}, u32[]{:S(2)}, u32[]{:S(2)}) %all-to-all-start) | async-done | bytes 1048608 | tf_op jit(solution)/shard_map/all_to_all | solution.py:162
  51.4 9.2 %all-to-all-start.1 = ((bf16[256,16,128]{2,0,1:T(8,128)(2,1)}), bf16[256,16,128]{2,0,1:T(8,128)(2,1)S(1)}, u32[]{:S(2)}, u32[]{:S(2)}) async-start(bf16[256,16,128]{2,0,1:T(8,128)(2,1)} %copy_bitcast_fusion.1), calls=%async_computation.1 | async-start | bytes 2097152 | tf_op jit(solution)/shard_map/all_to_all | solution.py:162
  60.7 2.5 copy_bitcast_fusion
  63.1 30.8 %all-to-all-done.1 = bf16[256,16,128]{2,0,1:T(8,128)(2,1)S(1)} async-done(((bf16[256,16,128]{2,0,1:T(8,128)(2,1)}), bf16[256,16,128]{2,0,1:T(8,128)(2,1)S(1)}, u32[]{:S(2)}, u32[]{:S(2)}) %all-to-all-start.1) | async-done | bytes 1048608 | tf_op jit(solution)/shard_map/all_to_all | solution.py:162
  93.9 6.9 %all-to-all-start.2 = ((bf16[256,16,128]{2,0,1:T(8,128)(2,1)}), bf16[256,16,128]{2,0,1:T(8,128)(2,1)}, u32[]{:S(2)}, u32[]{:S(2)}) async-start(bf16[256,16,128]{2,0,1:T(8,128)(2,1)} %copy_bitcast_fusion), calls=%async_computation.2 | async-start | bytes 2097152 | tf_op jit(solution)/shard_map/all_to_all | solution.py:162
  100.9 0.0 reduce-scatter.2.cloned.1.call-start
  100.9 0.8 select_reduce_fusion
  101.7 0.7 sub.18
  102.3 0.1 convert_reduce_fusion
  102.5 0.0 copy-done.1
  102.5 0.6 copy.17.qid_ref
  103.2 0.2 select_reduce_fusion.1
  103.4 0.2 select_reduce_fusion.2
  103.6 38.1 %all-to-all-done.2 = bf16[256,16,128]{2,0,1:T(8,128)(2,1)} async-done(((bf16[256,16,128]{2,0,1:T(8,128)(2,1)}), bf16[256,16,128]{2,0,1:T(8,128)(2,1)}, u32[]{:S(2)}, u32[]{:S(2)}) %all-to-all-start.2) | async-done | bytes 1048608 | tf_op jit(solution)/shard_map/all_to_all | solution.py:162
  141.6 1.2 copy-done.2
  142.9 1.2 copy-done.4
  144.1 25.8 %shard_map.55 = bf16[4096,128]{1,0:T(8,128)(2,1)S(1)} custom-call(s32[16]{0:T(128)S(1)} %get-tuple-element.6.low_ref, s32[16]{0:T(128)S(1)} %get-tuple-element.5.high_ref, bf16[4096,128]{1,0:T(8,128)(2,1)S(1)} %bitcast.32, bf16[4096,128]{1,0:T(8,128)(2,1)S(1)} %bitcast.33, bf16[4096,128]{1,0:T(8,128)(2,1)} %bitcast.5.v_ref, s32[4096,1]{1,0:T(8,128)S(1)} %copy.17.qid_ref, ...), custom_call_target="tpu_custom_call" | custom-call | flops 4294967296 | bytes 4194304 | tf_op jit(solution)/shard_map/pallas_call | solution.py:145
  169.9 0.0 copy-start.5
  169.9 1.0 copy-done.5
  170.9 1.5 copy.18
  172.4 64.3 %all_to_all.76 = bf16[16,256,128]{1,2,0:T(8,128)(2,1)S(1)} all-to-all(bf16[16,256,128]{1,2,0:T(8,128)(2,1)S(1)} %copy.18), channel_id=1, replica_groups=mesh['seq'=16,'tp'=2] {'seq'}, dimensions={0} | all-to-all | bytes 2097152 | tf_op jit(solution)/shard_map/all_to_all | solution.py:166
  236.7 73.9 %all-gather.2.cloned.1.call-done = bf16[2048,4096]{1,0:T(8,128)(2,1)} async-done(((bf16[2048,256]{1,0:T(8,128)(2,1)}), bf16[2048,4096]{1,0:T(8,128)(2,1)}) %all-gather.2.cloned.1.call-update) | async-done | bytes 16777232 | tf_op jit(solution)/shard_map/all_gather | solution.py:159
  310.6 11.5 %convolution_convert_fusion = bf16[256,4096]{1,0:T(8,128)(2,1)} fusion(bf16[256,2048]{0,1:T(8,128)(2,1)S(1)} %bitcast.37, bf16[2048,4096]{1,0:T(8,128)(2,1)} %all-gather.2.cloned.1.call-done), kind=kOutput, calls=%fused_computation | convolution fusion | flops 4296015872 | bytes 19922944 | tf_op jit(solution)/shard_map/dot_general | solution.py:169
  322.1 0.0 reduce-scatter.2.cloned.1.call-update
  322.1 11.3 %reduce-scatter.2.cloned.1.call-done = bf16[256,2048]{1,0:T(8,128)(2,1)} async-done(((bf16[256,4096]{1,0:T(8,128)(2,1)}), bf16[256,2048]{1,0:T(8,128)(2,1)}) %reduce-scatter.2.cloned.1.call-update) | async-done | bytes 1048592 | tf_op jit(solution)/shard_map/reduce_scatter | solution.py:170
  (8 shorter events, 0.0 us)
Async XLA Ops:
  6.5 1.2 copy-start
  6.5 304.0 %all-gather.2.cloned.1.call-start = ((), (), s32[]{:S(2)}) async-start(), calls=%async_computation.5 | async-start | bytes 17825792 | tf_op jit(solution)/shard_map/all_gather | solution.py:159
  9.0 42.4 %all-to-all-start = ((bf16[256,16,128]{2,0,1:T(8,128)(2,1)}), bf16[256,16,128]{2,0,1:T(8,128)(2,1)S(1)}, u32[]{:S(2)}, u32[]{:S(2)}) async-start(bf16[256,16,128]{2,0,1:T(8,128)(2,1)} %copy_bitcast_fusion.2), calls=%async_computation | async-start | bytes 2097152 | tf_op jit(solution)/shard_map/all_to_all | solution.py:162
  51.4 51.1 %copy-start.1 = (bf16[256,16,128]{2,0,1:T(8,128)(2,1)}, bf16[256,16,128]{2,0,1:T(8,128)(2,1)S(1)}, u32[]{:S(2)}) copy-start(bf16[256,16,128]{2,0,1:T(8,128)(2,1)S(1)} %all-to-all-done) | copy-start | bytes 3145732
  51.4 42.5 %all-to-all-start.1 = ((bf16[256,16,128]{2,0,1:T(8,128)(2,1)}), bf16[256,16,128]{2,0,1:T(8,128)(2,1)S(1)}, u32[]{:S(2)}, u32[]{:S(2)}) async-start(bf16[256,16,128]{2,0,1:T(8,128)(2,1)} %copy_bitcast_fusion.1), calls=%async_computation.1 | async-start | bytes 2097152 | tf_op jit(solution)/shard_map/all_to_all | solution.py:162
  93.9 8.6 %copy-start.3 = (bf16[256,16,128]{2,0,1:T(8,128)(2,1)}, bf16[256,16,128]{2,0,1:T(8,128)(2,1)S(1)}, u32[]{:S(2)}) copy-start(bf16[256,16,128]{2,0,1:T(8,128)(2,1)S(1)} %all-to-all-done.1) | copy-start | bytes 3145732
  93.9 47.7 %all-to-all-start.2 = ((bf16[256,16,128]{2,0,1:T(8,128)(2,1)}), bf16[256,16,128]{2,0,1:T(8,128)(2,1)}, u32[]{:S(2)}, u32[]{:S(2)}) async-start(bf16[256,16,128]{2,0,1:T(8,128)(2,1)} %copy_bitcast_fusion), calls=%async_computation.2 | async-start | bytes 2097152 | tf_op jit(solution)/shard_map/all_to_all | solution.py:162
  100.9 232.6 %reduce-scatter.2.cloned.1.call-start = ((), (), s32[]{:S(2)}) async-start(), calls=%async_computation.6 | async-start | bytes 3145728 | tf_op jit(solution)/shard_map/reduce_scatter | solution.py:170
  141.6 1.2 copy-start.2
  142.9 1.2 copy-start.4
  169.9 1.0 copy-start.5
Sparse Core Ops, SparseCore 0:
  10.1 300.4 all-gather.1
  322.3 11.1 reduce-scatter.1

commit v2 on v1

--- a/solution.py
+++ b/solution.py
@@ -9,6 +9,7 @@
 from jax.sharding import PartitionSpec as P
 
 HD = 128
+MESH = pl.DeviceIdType.MESH
 SCALE2 = math.log2(math.e) / math.sqrt(HD)
 
 
@@ -154,18 +155,267 @@
     )(low, high, q, k, v, ids[:, None], ids.reshape(tokens // bk, 1, bk))
 
 
-def local(parts, queries, keys, values, doc_lengths, out_weight):
-    heads_here = queries.shape[1] // HD
+def greet(parts, me, tp_too):
+    barrier = pltpu.get_barrier_semaphore()
+
+    @pl.loop(1, parts)
+    def _(step):
+        pl.semaphore_signal(
+            barrier, inc=1, device_id={"seq": lax.rem(me + step, parts)}, device_id_type=MESH
+        )
+
+    if tp_too:
+        other = 1 - lax.axis_index("tp")
+        pl.semaphore_signal(barrier, inc=1, device_id={"tp": other}, device_id_type=MESH)
+    pl.semaphore_wait(barrier, parts - 1 + int(tp_too))
+
+
+def spread_kernel(parts, q, k, v, q_out, k_out, v_out, send_sem, recv_sem, own_sem):
+    me = lax.axis_index("seq")
+    rows = q.shape[0]
+    width = q_out.shape[1]
+    pairs = ((q, q_out), (k, k_out), (v, v_out))
+
+    def columns(p):
+        return pl.ds(pl.multiple_of(p * width, width), width)
+
+    def place(p):
+        return pl.ds(pl.multiple_of(p * rows, rows), rows)
+
+    greet(parts, me, False)
+
+    @pl.loop(1, parts)
+    def _(step):
+        peer = lax.rem(me + step, parts)
+        for n, (src, dst) in enumerate(pairs):
+            pltpu.make_async_remote_copy(
+                src_ref=src.at[:, columns(peer)], dst_ref=dst.at[place(me), :],
+                send_sem=send_sem.at[n, peer], recv_sem=recv_sem.at[n, me],
+                device_id={"seq": peer}, device_id_type=MESH,
+            ).start()
+
+    owns = [
+        pltpu.make_async_copy(src.at[:, columns(me)], dst.at[place(me), :], own_sem.at[n])
+        for n, (src, dst) in enumerate(pairs)
+    ]
+    for own in owns:
+        own.start()
+    for own in owns:
+        own.wait()
+
+    @pl.loop(1, parts)
+    def _(step):
+        peer = lax.rem(me + step, parts)
+        source = lax.rem(me + parts - step, parts)
+        for n, (src, dst) in enumerate(pairs):
+            pltpu.make_async_remote_copy(
+                src_ref=src.at[:, columns(peer)], dst_ref=dst.at[place(source), :],
+                send_sem=send_sem.at[n, peer], recv_sem=recv_sem.at[n, source],
+                device_id={"seq": peer}, device_id_type=MESH,
+            ).wait()
+
+
+def spread(parts, q, k, v):
+    rows, features = q.shape
+    shape = jax.ShapeDtypeStruct((rows * parts, features // parts), q.dtype)
+    return pl.pallas_call(
+        functools.partial(spread_kernel, parts),
+        out_shape=[shape] * 3,
+        in_specs=[pl.BlockSpec(memory_space=pl.ANY)] * 3,
+        out_specs=[pl.BlockSpec(memory_space=pl.ANY)] * 3,
+        scratch_shapes=[
+            pltpu.SemaphoreType.DMA((3, parts)),
+            pltpu.SemaphoreType.DMA((3, parts)),
+            pltpu.SemaphoreType.DMA((3,)),
+        ],
+        compiler_params=pltpu.CompilerParams(collective_id=0, has_side_effects=True),
+        cost_estimate=pl.CostEstimate(flops=0, bytes_accessed=q.size * 200, transcendentals=0),
+    )(q, k, v)
+
+
+def back_kernel(parts, group, mixed, out, send_sem, recv_sem, pass_sem, got_sem, own_sem):
+    me = lax.axis_index("seq")
+    width = mixed.shape[1]
+    rows = mixed.shape[0] // parts
+    mine = lax.rem(me, group)
+    base = me - mine
+
+    def block(member, source):
+        return out.at[
+            pl.ds(pl.multiple_of(member * rows, rows), rows),
+            pl.ds(pl.multiple_of(source * width, width), width),
+        ]
+
+    def send(peer, source):
+        return pltpu.make_async_remote_copy(
+            src_ref=mixed.at[pl.ds(pl.multiple_of(peer * rows, rows), rows), :],
+            dst_ref=block(lax.rem(peer, group), me),
+            send_sem=send_sem.at[peer], recv_sem=recv_sem.at[me],
+            device_id={"seq": peer}, device_id_type=MESH,
+        )
+
+    def hand_on(far, source):
+        member = lax.rem(mine + far, group)
+        return pltpu.make_async_remote_copy(
+            src_ref=block(mine, source), dst_ref=block(mine, source),
+            send_sem=pass_sem.at[member, source], recv_sem=got_sem.at[mine, source],
+            device_id={"seq": base + member}, device_id_type=MESH,
+        )
+
+    greet(parts, me, False)
+
+    @pl.loop(1, parts)
+    def _(step):
+        send(lax.rem(me + step, parts), me).start()
+
+    own = pltpu.make_async_copy(
+        mixed.at[pl.ds(pl.multiple_of(me * rows, rows), rows), :], block(mine, me), own_sem
+    )
+    own.start()
+    own.wait()
+    for far in range(1, group):
+        hand_on(far, me).start()
+
+    @pl.loop(1, parts)
+    def _(step):
+        source = lax.rem(me + parts - step, parts)
+        pltpu.make_async_remote_copy(
+            src_ref=block(mine, source), dst_ref=block(mine, source),
+            send_sem=send_sem.at[source], recv_sem=recv_sem.at[source],
+            device_id={"seq": source}, device_id_type=MESH,
+        ).wait_recv()
+        for far in range(1, group):
+            hand_on(far, source).start()
+
+    @pl.loop(1, parts)
+    def _(step):
+        send(lax.rem(me + step, parts), me).wait_send()
+
+    @pl.loop(0, parts)
+    def _(source):
+        for far in range(1, group):
+            hand_on(far, source).wait_send()
+            member = lax.rem(mine + far, group)
+            pltpu.make_async_remote_copy(
+                src_ref=block(member, source), dst_ref=block(member, source),
+                send_sem=pass_sem.at[member, source], recv_sem=got_sem.at[member, source],
+                device_id={"seq": base + member}, device_id_type=MESH,
+            ).wait_recv()
+
+
+def back(parts, group, mixed):
+    tokens, width = mixed.shape
+    return pl.pallas_call(
+        functools.partial(back_kernel, parts, group),
+        out_shape=jax.ShapeDtypeStruct((tokens // parts * group, width * parts), mixed.dtype),
+        in_specs=[pl.BlockSpec(memory_space=pl.ANY)],
+        out_specs=pl.BlockSpec(memory_space=pl.ANY),
+        scratch_shapes=[
+            pltpu.SemaphoreType.DMA((parts,)),
+            pltpu.SemaphoreType.DMA((parts,)),
+            pltpu.SemaphoreType.DMA((group, parts)),
+            pltpu.SemaphoreType.DMA((group, parts)),
+            pltpu.SemaphoreType.DMA,
+        ],
+        compiler_params=pltpu.CompilerParams(collective_id=1, has_side_effects=True),
+        cost_estimate=pl.CostEstimate(flops=0, bytes_accessed=mixed.size * 200, transcendentals=0),
+    )(mixed)
+
+
+def home_kernel(parts, group, part, out, came, summed, tp_send, tp_recv, send_sem, recv_sem):
+    me = lax.axis_index("seq")
+    half = lax.axis_index("tp")
+    mine = lax.rem(me, group)
+    base = me - mine
+    rows, features = out.shape
+    span = came.shape[2]
+    piece = features // parts * 2
+    runs = span // piece
+
+    def keep(which):
+        return pl.ds(pl.multiple_of(which * span, span), span)
+
+    def swap(member):
+        return pltpu.make_async_remote_copy(
+            src_ref=part.at[pl.ds(pl.multiple_of(member * rows, rows), rows), keep(1 - half)],
+            dst_ref=came.at[member],
+            send_sem=tp_send.at[member], recv_sem=tp_recv.at[member],
+            device_id={"tp": 1 - half}, device_id_type=MESH,
+        )
+
+    def target(member, run):
+        at = (run * group + member) * piece
+        return out.at[:, pl.ds(pl.multiple_of(at, piece), piece)]
+
+    def send(member, run, to, sem):
+        return pltpu.make_async_remote_copy(
+            src_ref=summed.at[member, :, pl.ds(run * piece, piece)], dst_ref=target(sem, run),
+            send_sem=send_sem.at[member, run], recv_sem=recv_sem.at[sem, run],
+            device_id={"seq": to}, device_id_type=MESH,
+        )
+
+    greet(parts, me, True)
+    order = [lax.rem(mine + far, group) for far in (*range(1, group), 0)]
+    for member in order:
+        swap(member).start()
+    for member in order:
+        swap(member).wait_recv()
+        own = part[pl.ds(pl.multiple_of(member * rows, rows), rows), keep(half)]
+        total = own.astype(jnp.float32) + came[member].astype(jnp.float32)
+        if member is order[-1]:
+            for run in range(runs):
+                at = pl.multiple_of((run * group + mine) * piece, piece)
+                out[:, pl.ds(at, piece)] = total[:, run * piece:(run + 1) * piece].astype(out.dtype)
+        else:
+            summed[member] = total.astype(summed.dtype)
+            for run in range(runs):
+                send(member, run, base + member, mine).start()
+    for member in order[:-1]:
+        for run in range(runs):
+            send(member, run, base + member, mine).wait_send()
+            send(member, run, base + member, member).wait_recv()
+    for member in order:
+        swap(member).wait_send()
+
+
+def home(parts, group, rows, part):
+    tall, wide = part.shape
+    span = wide // 2
+    features = span * group
+    return pl.pallas_call(
+        functools.partial(home_kernel, parts, group),
+        out_shape=jax.ShapeDtypeStruct((rows, features), part.dtype),
+        in_specs=[pl.BlockSpec(memory_space=pltpu.VMEM)],
+        out_specs=pl.BlockSpec(memory_space=pltpu.VMEM),
+        scratch_shapes=[
+            pltpu.VMEM((group, rows, span), part.dtype),
+            pltpu.VMEM((group, rows, span), part.dtype),
+            pltpu.SemaphoreType.DMA((group,)),
+            pltpu.SemaphoreType.DMA((group,)),
+            pltpu.SemaphoreType.DMA((group, parts // group // 2)),
+            pltpu.SemaphoreType.DMA((group, parts // group // 2)),
+        ],
+        compiler_params=pltpu.CompilerParams(
+            collective_id=2, has_side_effects=True, vmem_limit_bytes=24 << 20
+        ),
+    )(part)
+
+
+def local(parts, pair, queries, keys, values, doc_lengths, out_weight):
+    rows, width = queries.shape
+    group = math.isqrt(parts)
+    if pair == 2 and group * group == parts and group % 2 == 0 and width // HD % parts == 0:
+        across = [[m + group * n for n in range(group)] for m in range(group)]
+        weight = lax.all_gather(
+            out_weight, "seq", axis=1, tiled=True, axis_index_groups=across
+        )
+        q, k, v = spread(parts, queries, keys, values)
+        mixed = attend_heads(q, k, v, doc_lengths)
+        attended = back(parts, group, mixed)
+        part = jnp.dot(attended, weight, preferred_element_type=jnp.float32)
+        return home(parts, group, rows, part.astype(jnp.bfloat16))
     weight = lax.all_gather(out_weight, "seq", axis=1, tiled=True)
-    if heads_here % parts == 0:
-        q, k, v = [
-            lax.all_to_all(a, "seq", split_axis=1, concat_axis=0, tiled=True)
-            for a in (queries, keys, values)
-        ]
-        mixed = attend_heads(q, k, v, doc_lengths)
-        attended = lax.all_to_all(mixed, "seq", split_axis=0, concat_axis=1, tiled=True)
-    else:
-        attended = attend_gathered(queries, keys, values, doc_lengths)
+    attended = attend_gathered(queries, keys, values, doc_lengths)
     partial_value = jnp.dot(attended, weight, preferred_element_type=jnp.float32)
     return lax.psum_scatter(
         partial_value.astype(jnp.bfloat16), "tp", scatter_dimension=1, tiled=True
@@ -176,6 +426,6 @@
     in_specs = (P("seq", "tp"), P("seq", "tp"), P("seq", "tp"), P(), P("tp", "seq"))
     out_specs = P("seq", "tp")
     return jax.shard_map(
-        functools.partial(local, mesh.shape["seq"]),
+        functools.partial(local, mesh.shape["seq"], mesh.shape["tp"]),
         mesh=mesh, in_specs=in_specs, out_specs=out_specs, check_vma=False,
     )

time: 341 us -> 287 us (0.84)
  Pallas kernels: 25.8 us -> 254 us
  waiting for transfers between devices: 188 us -> 0.73 us
  blocking collectives: 64.3 us -> 0 us
  starting transfers between devices: 22.7 us -> 0.01 us
  local copies, waits for them, and re-layouts: 12.3 us -> 6.24 us
  matrix products: 11.5 us -> 7.95 us
    pallas_call x0 -> x3, Pallas kernels: none -> 223 us  [the longest x1 105 us: back(): pl.pallas_call(functools.partial(back_kernel, parts, group), out_shape=ja...]
    all_to_all x3 -> x0, waiting for transfers between devices: 102 us -> none  [local(): lax.all_to_all(a, 'seq', split_axis=1, concat_axis=0, tiled=True)]
    all_gather x1, waiting for transfers between devices: 73.9 us -> 0.02 us  [local(): lax.all_gather(out_weight, 'seq', axis=1, tiled=True, axis_index_groups=a...]
    all_to_all x1 -> x0, blocking collectives: 64.3 us -> none  [local(): lax.all_to_all(mixed, 'seq', split_axis=0, concat_axis=1, tiled=True)]
    all_to_all x3 -> x0, starting transfers between devices: 22.6 us -> none  [local(): lax.all_to_all(a, 'seq', split_axis=1, concat_axis=0, tiled=True)]
    reduce_scatter x1 -> x0, waiting for transfers between devices: 11.3 us -> none  [local(): lax.psum_scatter(partial_value.astype(jnp.bfloat16), 'tp', scatter_dimens...]
    all_to_all x4 -> x0, local copies, waits for them, and re-layouts: 7.69 us -> none  [the longest x3 6.21 us: local(): lax.all_to_all(a, 'seq', split_axis=1, concat_axis=0, tiled=True)]
    pallas_call x1, Pallas kernels: 25.8 us -> 30.7 us  [attend_heads(): pl.pallas_call(functools.partial(attend_kernel, bk), out_shape=jax.ShapeD...]
  transfers between devices with their start and end apart: 5 -> 1, of which waited for: 5 -> 0; matrix products, arithmetic and copies ran while one was open for 3% -> 1% of each run, Pallas kernels for 8% -> 83%
where the time goes in v2:
time: 287 us; the launch traced here: 284 us
  Pallas kernels  254 us (89%)
  between operations  13.5 us (5%)
  matrix products  7.95 us (3%)
  local copies, waits for them, and re-layouts  6.24 us (2%)
    pallas_call x1, Pallas kernels, back(): pl.pallas_call(functools.partial(back_kernel, parts, group), out_shape=ja...  105 us
    pallas_call x1, Pallas kernels, spread(): pl.pallas_call(functools.partial(spread_kernel, parts), out_shape=[shape]...  99.5 us
    pallas_call x1, Pallas kernels, attend_heads(): pl.pallas_call(functools.partial(attend_kernel, bk), out_shape=jax.ShapeD...  30.7 us
    pallas_call x1, Pallas kernels, home(): pl.pallas_call(functools.partial(home_kernel, parts, group), out_shape=ja...  18.7 us
    dot_general x1, matrix products, local(): part = jnp.dot(attended, weight, preferred_element_type=jnp.float32)  7.95 us
  transfers between devices with their start and end apart: 1, of which 0 were waited for; matrix products, arithmetic and copies ran while one was open for 1% of the time, Pallas kernels for 83%

profile of v2, /device:TPU:25, one launch (start us, length us, event | category | flops | bytes accessed | tf_op | source)
XLA Modules:
  0.0 284.1 jit_solution(8186385005664543072)
XLA Ops:
  6.5 0.0 all-gather.2.cloned.1.call-start
  6.5 0.7 all-gather.2.cloned.1.call-update
  7.3 0.8 select_reduce_fusion
  8.0 0.7 sub.18
  8.7 0.1 convert_reduce_fusion
  8.8 0.6 copy.7.qid_ref
  9.5 99.5 %shard_map.55 = (bf16[4096,128]{1,0:T(8,128)(2,1)}, bf16[4096,128]{1,0:T(8,128)(2,1)}, bf16[4096,128]{1,0:T(8,128)(2,1)}) custom-call(bf16[256,2048]{1,0:T(8,128)(2,1)} %q.1, bf16[256,2048]{1,0:T(8,128)(2,1)} %k.1, bf16[256,2048]{1,0:T(8,128)(2,1)} %v.1), custom_call_target="tpu_custom_call" | custom-call | bytes 104857600 | tf_op jit(solution)/shard_map/pallas_call | solution.py:221
  109.1 0.2 select_reduce_fusion.1
  109.3 0.2 select_reduce_fusion.2
  109.5 0.0 copy-start.1
  109.5 1.2 copy-done.1
  110.7 0.0 copy-start.2
  110.7 1.2 copy-done.2
  111.9 0.0 copy-start.3
  111.9 1.2 copy-done.3
  113.1 30.7 %shard_map.56.mixed = bf16[4096,128]{1,0:T(8,128)(2,1)S(1)} custom-call(s32[16]{0:T(128)S(1)} %get-tuple-element.12.low_ref, s32[16]{0:T(128)S(1)} %get-tuple-element.11.high_ref, bf16[4096,128]{1,0:T(8,128)(2,1)S(1)} %copy-done.1, bf16[4096,128]{1,0:T(8,128)(2,1)S(1)} %copy-done.2, bf16[4096,128]{1,0:T(8,128)(2,1)S(1)} %copy-done.3, ...), custom_call_target="tpu_custom_call" | custom-call | flops 4294967296 | bytes 4194304 | tf_op jit(solution)/shard_map/pallas_call | solution.py:146
  143.8 0.0 copy-start
  143.8 1.0 copy-done
  144.8 104.8 %shard_map.57 = bf16[1024,2048]{1,0:T(8,128)(2,1)} custom-call(bf16[4096,128]{1,0:T(8,128)(2,1)} %copy-done), custom_call_target="tpu_custom_call" | custom-call | bytes 104857600 | tf_op jit(solution)/shard_map/pallas_call | solution.py:308
  249.6 0.0 all-gather.2.cloned.1.call-done
  249.6 8.0 %convolution_convert_fusion.part = bf16[1024,1024]{1,0:T(8,128)(2,1)S(1)} fusion(bf16[1024,2048]{1,0:T(8,128)(2,1)} %shard_map.57, bf16[2048,1024]{1,0:T(8,128)(2,1)} %all-gather.2.cloned.1.call-done), kind=kOutput, calls=%fused_computation | convolution fusion | flops 4296015872 | bytes 10485760 | tf_op jit(solution)/shard_map/dot_general | solution.py:415
  257.6 18.7 %shard_map.58 = bf16[256,2048]{1,0:T(8,128)(2,1)S(1)} custom-call(bf16[1024,1024]{1,0:T(8,128)(2,1)S(1)} %convolution_convert_fusion.part), custom_call_target="tpu_custom_call" | custom-call | tf_op jit(solution)/shard_map/pallas_call | solution.py:385
  276.3 1.0 copy.9
  (3 shorter events, 0.0 us)
Async XLA Ops:
  6.5 243.1 %all-gather.2.cloned.1.call-start = ((), (), s32[]{:S(2)}) async-start(), calls=%async_computation | async-start | bytes 5242880 | tf_op jit(solution)/shard_map/all_gather | solution.py:409
  109.5 1.2 copy-start.1
  110.7 1.2 copy-start.2
  111.9 1.2 copy-start.3
  143.8 1.0 copy-start
Sparse Core Ops, SparseCore 0:
  8.9 142.4 all-gather.1

commit v3 on v2

--- a/solution.py
+++ b/solution.py
@@ -155,7 +155,7 @@
     )(low, high, q, k, v, ids[:, None], ids.reshape(tokens // bk, 1, bk))
 
 
-def greet(parts, me, tp_too):
+def greet(parts, me):
     barrier = pltpu.get_barrier_semaphore()
 
     @pl.loop(1, parts)
@@ -164,10 +164,7 @@
             barrier, inc=1, device_id={"seq": lax.rem(me + step, parts)}, device_id_type=MESH
         )
 
-    if tp_too:
-        other = 1 - lax.axis_index("tp")
-        pl.semaphore_signal(barrier, inc=1, device_id={"tp": other}, device_id_type=MESH)
-    pl.semaphore_wait(barrier, parts - 1 + int(tp_too))
+    pl.semaphore_wait(barrier, parts - 1)
 
 
 def spread_kernel(parts, q, k, v, q_out, k_out, v_out, send_sem, recv_sem, own_sem):
@@ -182,7 +179,7 @@
     def place(p):
         return pl.ds(pl.multiple_of(p * rows, rows), rows)
 
-    greet(parts, me, False)
+    greet(parts, me)
 
     @pl.loop(1, parts)
     def _(step):
@@ -262,7 +259,7 @@
             device_id={"seq": base + member}, device_id_type=MESH,
         )
 
-    greet(parts, me, False)
+    greet(parts, me)
 
     @pl.loop(1, parts)
     def _(step):
@@ -354,7 +351,14 @@
             device_id={"seq": to}, device_id_type=MESH,
         )
 
-    greet(parts, me, True)
+    barrier = pltpu.get_barrier_semaphore()
+    pl.semaphore_signal(barrier, inc=1, device_id={"tp": 1 - half}, device_id_type=MESH)
+    for far in range(1, group):
+        pl.semaphore_signal(
+            barrier, inc=1, device_id={"seq": base + lax.rem(mine + far, group)},
+            device_id_type=MESH,
+        )
+    pl.semaphore_wait(barrier, group)
     order = [lax.rem(mine + far, group) for far in (*range(1, group), 0)]
     for member in order:
         swap(member).start()
@@ -406,10 +410,11 @@
     group = math.isqrt(parts)
     if pair == 2 and group * group == parts and group % 2 == 0 and width // HD % parts == 0:
         across = [[m + group * n for n in range(group)] for m in range(group)]
+        q, k, v = spread(parts, queries, keys, values)
+        q, out_weight = lax.optimization_barrier((q, out_weight))
         weight = lax.all_gather(
             out_weight, "seq", axis=1, tiled=True, axis_index_groups=across
         )
-        q, k, v = spread(parts, queries, keys, values)
         mixed = attend_heads(q, k, v, doc_lengths)
         attended = back(parts, group, mixed)
         part = jnp.dot(attended, weight, preferred_element_type=jnp.float32)

time: 287 us -> 235 us (0.82); the launches traced: 284 us -> 235 us
  Pallas kernels: 254 us -> 207 us
    pallas_call x1, Pallas kernels: 99.5 us -> 65.7 us  [spread(): pl.pallas_call(functools.partial(spread_kernel, parts), out_shape=[shape]...]
    pallas_call x1, Pallas kernels: 105 us -> 92 us  [back(): pl.pallas_call(functools.partial(back_kernel, parts, group), out_shape=ja...]
  transfers between devices with their start and end apart: 1 -> 1, of which waited for: 0 -> 0; matrix products, arithmetic and copies ran while one was open for 1% -> 1% of each run, Pallas kernels for 83% -> 52%
where the time goes in v3:
time: 235 us
  Pallas kernels  207 us (88%)
  between operations  13.5 us (6%)
  matrix products  7.95 us (3%)
  local copies, waits for them, and re-layouts  6.25 us (3%)
    pallas_call x1, Pallas kernels, back(): pl.pallas_call(functools.partial(back_kernel, parts, group), out_shape=ja...  92 us
    pallas_call x1, Pallas kernels, spread(): pl.pallas_call(functools.partial(spread_kernel, parts), out_shape=[shape]...  65.7 us
    pallas_call x1, Pallas kernels, attend_heads(): pl.pallas_call(functools.partial(attend_kernel, bk), out_shape=jax.ShapeD...  30.6 us
    pallas_call x1, Pallas kernels, home(): pl.pallas_call(functools.partial(home_kernel, parts, group), out_shape=ja...  18.5 us
    dot_general x1, matrix products, local(): part = jnp.dot(attended, weight, preferred_element_type=jnp.float32)  7.95 us
    unnamed x11, local copies, waits for them, and re-layouts  5.61 us
  transfers between devices with their start and end apart: 1, of which 0 were waited for; matrix products, arithmetic and copies ran while one was open for 1% of the time, Pallas kernels for 52%

profile of v3, /device:TPU:25, one launch (start us, length us, event | category | flops | bytes accessed | tf_op | source)
XLA Modules:
  0.0 235.2 jit_solution(9499428557314990275)
XLA Ops:
  6.5 0.0 copy-start.4
  6.5 0.0 all-gather.2.cloned.1.call-start
  6.5 65.7 %shard_map.55 = (bf16[4096,128]{1,0:T(8,128)(2,1)}, bf16[4096,128]{1,0:T(8,128)(2,1)}, bf16[4096,128]{1,0:T(8,128)(2,1)}) custom-call(bf16[256,2048]{1,0:T(8,128)(2,1)} %q.1, bf16[256,2048]{1,0:T(8,128)(2,1)} %k.1, bf16[256,2048]{1,0:T(8,128)(2,1)} %v.1), custom_call_target="tpu_custom_call" | custom-call | bytes 104857600 | tf_op jit(solution)/shard_map/pallas_call | solution.py:218
  72.3 0.0 all-gather.2.cloned.1.call-update
  72.3 0.0 copy-done.4
  72.3 0.1 select_reduce_fusion
  72.5 0.1 convert_reduce_fusion
  72.6 0.6 copy.7.qid_ref
  73.3 0.2 select_reduce_fusion.1
  73.5 0.2 select_reduce_fusion.2
  73.7 0.0 copy-start.1
  73.7 1.2 copy-done.1
  74.9 0.0 copy-start.2
  74.9 1.2 copy-done.2
  76.1 0.0 copy-start.3
  76.1 1.2 copy-done.3
  77.3 30.6 %shard_map.56.mixed = bf16[4096,128]{1,0:T(8,128)(2,1)S(1)} custom-call(s32[16]{0:T(128)S(1)} %get-tuple-element.16.low_ref, s32[16]{0:T(128)S(1)} %get-tuple-element.15.high_ref, bf16[4096,128]{1,0:T(8,128)(2,1)S(1)} %copy-done.1, bf16[4096,128]{1,0:T(8,128)(2,1)S(1)} %copy-done.2, bf16[4096,128]{1,0:T(8,128)(2,1)S(1)} %copy-done.3, ...), custom_call_target="tpu_custom_call" | custom-call | flops 4294967296 | bytes 4194304 | tf_op jit(solution)/shard_map/pallas_call | solution.py:146
  108.0 0.0 copy-start
  108.0 1.0 copy-done
  108.9 92.0 %shard_map.57 = bf16[1024,2048]{1,0:T(8,128)(2,1)} custom-call(bf16[4096,128]{1,0:T(8,128)(2,1)} %copy-done), custom_call_target="tpu_custom_call" | custom-call | bytes 104857600 | tf_op jit(solution)/shard_map/pallas_call | solution.py:305
  200.9 0.0 all-gather.2.cloned.1.call-done
  200.9 8.0 %convolution_convert_fusion.part = bf16[1024,1024]{1,0:T(8,128)(2,1)S(1)} fusion(bf16[1024,2048]{1,0:T(8,128)(2,1)} %shard_map.57, bf16[2048,1024]{1,0:T(8,128)(2,1)} %all-gather.2.cloned.1.call-done), kind=kOutput, calls=%fused_computation | convolution fusion | flops 4296015872 | bytes 10485760 | tf_op jit(solution)/shard_map/dot_general | solution.py:420
  208.9 18.5 %shard_map.58 = bf16[256,2048]{1,0:T(8,128)(2,1)S(1)} custom-call(bf16[1024,1024]{1,0:T(8,128)(2,1)S(1)} %convolution_convert_fusion.part), custom_call_target="tpu_custom_call" | custom-call | tf_op jit(solution)/shard_map/pallas_call | solution.py:389
  227.4 1.0 copy.9
  (4 shorter events, 0.0 us)
Async XLA Ops:
  6.5 65.8 %copy-start.4 = (s32[32]{0:T(128)S(1)}, s32[32]{0:T(128)}, u32[]{:S(2)}) copy-start(s32[32]{0:T(128)} %param.8) | copy-start | bytes 388
  6.5 194.4 %all-gather.2.cloned.1.call-start = ((), (), s32[]{:S(2)}) async-start(), calls=%async_computation | async-start | bytes 5242880 | tf_op jit(solution)/shard_map/all_gather | solution.py:415
  73.7 1.2 copy-start.1
  74.9 1.2 copy-start.2
  76.1 1.2 copy-start.3
  108.0 1.0 copy-start
Sparse Core Ops, SparseCore 0:
  72.4 114.5 all-gather.1

commit v4 on v3

--- a/solution.py
+++ b/solution.py
@@ -122,7 +122,7 @@
 
 def attend_heads(q, k, v, doc_lengths):
     tokens, width = q.shape
-    bq = math.gcd(tokens, 256)
+    bq = math.gcd(tokens, 512)
     bk = math.gcd(tokens, 512)
     ids = doc_of(jnp.arange(tokens, dtype=jnp.int32), doc_lengths)
     ends = ends_of(doc_lengths)

time: 235 us -> 235 us (level)
    pallas_call x1, Pallas kernels: 92 us -> 95.5 us  [back(): pl.pallas_call(functools.partial(back_kernel, parts, group), out_shape=ja...]
    pallas_call x1, Pallas kernels: 30.6 us -> 27.2 us  [attend_heads(): pl.pallas_call(functools.partial(attend_kernel, bk), out_shape=jax.ShapeD...]
where the time goes in v4:
time: 235 us
  Pallas kernels  207 us (88%)
  between operations  13.5 us (6%)
  matrix products  7.95 us (3%)
  local copies, waits for them, and re-layouts  6.25 us (3%)
    pallas_call x1, Pallas kernels, back(): pl.pallas_call(functools.partial(back_kernel, parts, group), out_shape=ja...  95.5 us
    pallas_call x1, Pallas kernels, spread(): pl.pallas_call(functools.partial(spread_kernel, parts), out_shape=[shape]...  65.7 us
    pallas_call x1, Pallas kernels, attend_heads(): pl.pallas_call(functools.partial(attend_kernel, bk), out_shape=jax.ShapeD...  27.2 us
    pallas_call x1, Pallas kernels, home(): pl.pallas_call(functools.partial(home_kernel, parts, group), out_shape=ja...  18.4 us
    dot_general x1, matrix products, local(): part = jnp.dot(attended, weight, preferred_element_type=jnp.float32)  7.95 us
    unnamed x11, local copies, waits for them, and re-layouts  5.61 us
  transfers between devices with their start and end apart: 1, of which 0 were waited for; matrix products, arithmetic and copies ran while one was open for 1% of the time, Pallas kernels for 52%

profile of v4, /device:TPU:25, one launch (start us, length us, event | category | flops | bytes accessed | tf_op | source)
XLA Modules:
  0.0 235.2 jit_solution(4611991347460392727)
XLA Ops:
  6.5 0.0 copy-start.4
  6.5 0.0 all-gather.2.cloned.1.call-start
  6.5 65.7 %shard_map.55 = (bf16[4096,128]{1,0:T(8,128)(2,1)}, bf16[4096,128]{1,0:T(8,128)(2,1)}, bf16[4096,128]{1,0:T(8,128)(2,1)}) custom-call(bf16[256,2048]{1,0:T(8,128)(2,1)} %q.1, bf16[256,2048]{1,0:T(8,128)(2,1)} %k.1, bf16[256,2048]{1,0:T(8,128)(2,1)} %v.1), custom_call_target="tpu_custom_call" | custom-call | bytes 104857600 | tf_op jit(solution)/shard_map/pallas_call | solution.py:218
  72.3 0.0 all-gather.2.cloned.1.call-update
  72.3 0.0 copy-done.4
  72.3 0.1 select_reduce_fusion
  72.5 0.1 convert_reduce_fusion
  72.6 0.6 copy.7.qid_ref
  73.3 0.2 select_reduce_fusion.1
  73.5 0.2 select_reduce_fusion.2
  73.7 0.0 copy-start.1
  73.7 1.2 copy-done.1
  74.9 0.0 copy-start.2
  74.9 1.2 copy-done.2
  76.1 0.0 copy-start.3
  76.1 1.2 copy-done.3
  77.3 27.2 %shard_map.56.mixed = bf16[4096,128]{1,0:T(8,128)(2,1)S(1)} custom-call(s32[8]{0:T(128)S(1)} %get-tuple-element.16.low_ref, s32[8]{0:T(128)S(1)} %get-tuple-element.15.high_ref, bf16[4096,128]{1,0:T(8,128)(2,1)S(1)} %copy-done.1, bf16[4096,128]{1,0:T(8,128)(2,1)S(1)} %copy-done.2, bf16[4096,128]{1,0:T(8,128)(2,1)S(1)} %copy-done.3, ...), custom_call_target="tpu_custom_call" | custom-call | flops 4294967296 | bytes 4194304 | tf_op jit(solution)/shard_map/pallas_call | solution.py:146
  104.5 0.0 copy-start
  104.5 1.0 copy-done
  105.5 95.5 %shard_map.57 = bf16[1024,2048]{1,0:T(8,128)(2,1)} custom-call(bf16[4096,128]{1,0:T(8,128)(2,1)} %copy-done), custom_call_target="tpu_custom_call" | custom-call | bytes 104857600 | tf_op jit(solution)/shard_map/pallas_call | solution.py:305
  201.0 0.0 all-gather.2.cloned.1.call-done
  201.0 8.0 %convolution_convert_fusion.part = bf16[1024,1024]{1,0:T(8,128)(2,1)S(1)} fusion(bf16[1024,2048]{1,0:T(8,128)(2,1)} %shard_map.57, bf16[2048,1024]{1,0:T(8,128)(2,1)} %all-gather.2.cloned.1.call-done), kind=kOutput, calls=%fused_computation | convolution fusion | flops 4296015872 | bytes 10485760 | tf_op jit(solution)/shard_map/dot_general | solution.py:420
  209.0 18.4 %shard_map.58 = bf16[256,2048]{1,0:T(8,128)(2,1)S(1)} custom-call(bf16[1024,1024]{1,0:T(8,128)(2,1)S(1)} %convolution_convert_fusion.part), custom_call_target="tpu_custom_call" | custom-call | tf_op jit(solution)/shard_map/pallas_call | solution.py:389
  227.4 1.0 copy.9
  (4 shorter events, 0.0 us)
Async XLA Ops:
  6.5 65.8 %copy-start.4 = (s32[32]{0:T(128)S(1)}, s32[32]{0:T(128)}, u32[]{:S(2)}) copy-start(s32[32]{0:T(128)} %param.8) | copy-start | bytes 388
  6.5 194.5 %all-gather.2.cloned.1.call-start = ((), (), s32[]{:S(2)}) async-start(), calls=%async_computation | async-start | bytes 5242880 | tf_op jit(solution)/shard_map/all_gather | solution.py:415
  73.7 1.2 copy-start.1
  74.9 1.2 copy-start.2
  76.1 1.2 copy-start.3
  104.5 1.0 copy-start
Sparse Core Ops, SparseCore 0:
  72.4 114.5 all-gather.1
